TPU v7x, 256 devices: a whole 4x4x8 slice. The times are simulated.
256 devices in a mesh: grid: 64 (over x_lo, z, y), orb: 4 (over x_hi, core).
Axes of the slice: x: 4 (x_hi: 2, x_lo: 2; x = x_hi * 2 + x_lo), y: 4, z: 8, core: 2. Of those that a mesh axis runs over, the one named last changes fastest.
Arguments:
- orbitals: float32 [16, 512, 32, 128], P('orb', 'grid'), may hold values from -6 to 6
- potential: float32 [512, 32, 128], P('grid'), may hold values from -1 to 1
Outputs:
- filtered: float32 [16, 512, 32, 128], P('orb', 'grid')
- correlation: float32 [16, 16], P('orb')
- hamiltonian: float32 [16, 16], P('orb')
All inputs are finite; a program needn't handle non-finite values.
Results may differ from a plain program's by a relative error of at most 0.00005.
Values sent between devices are 32-bit elements; how exact they have to be, the bound alone decides.
A program may use at most 64 MiB of HBM per device.

v0:
```python
import jax
import jax.numpy as jnp
from jax import lax
from jax.sharding import PartitionSpec as P

COEFS = (-205.0 / 72.0, 8.0 / 5.0, -1.0 / 5.0, 8.0 / 315.0, -1.0 / 560.0)
LOWER = -1.0
CUT = 4.0
UPPER = 10.0


def padded_2(value, sides, width):
    for axis, dim in sides:
        size, length = (lax.axis_size(axis), value.shape[dim])
        up = [(i, (i + 1) % size) for i in range(size)]
        down = [(j, i) for i, j in up]
        last = lax.slice_in_dim(value, length - width, length, axis=dim)
        first = lax.slice_in_dim(value, 0, width, axis=dim)
        before = lax.ppermute(last, axis, up)
        after = lax.ppermute(first, axis, down)
        value = jnp.concatenate([before, value, after], axis=dim)
    return value


def apply_ham(field, potential):
    width = field.shape[1]
    padded = padded_2(field, (("grid", 1),), 4)
    lap = 3.0 * COEFS[0] * field
    for shift_by in range(1, 5):
        lap = lap + COEFS[shift_by] * (
            padded[:, 4 + shift_by : 4 + shift_by + width]
            + padded[:, 4 - shift_by : 4 - shift_by + width]
        )
    for axis_pos in (2, 3):
        for shift_by in range(1, 5):
            lap = lap + COEFS[shift_by] * (
                jnp.roll(field, shift_by, axis_pos) + jnp.roll(field, -shift_by, axis_pos)
            )
    return -0.5 * lap + potential[None] * field


def cell_product(left, right):
    return lax.dot_general(left, right, (((1,), (1,)), ((), ())), precision=lax.Precision.HIGHEST)


def per_device(orbitals, potential):
    half = (UPPER - CUT) / 2.0
    centre = (UPPER + CUT) / 2.0
    first_sigma = half / (LOWER - centre)
    previous = orbitals
    current = (apply_ham(orbitals, potential) - centre * orbitals) * (first_sigma / half)
    sigma = first_sigma
    for step in range(3):
        sigma_new = 1.0 / (2.0 / first_sigma - sigma)
        following = (
            2.0 * sigma_new / half * (apply_ham(current, potential) - centre * current)
            - sigma * sigma_new * previous
        )
        previous = current
        current = following
        sigma = sigma_new
    applied = apply_ham(current, potential)
    own = current.shape[0]
    cells = current.shape[1] * lax.axis_size("grid") * current.shape[2] * current.shape[3]
    mine_y = current.reshape(own, -1)
    mine_h = applied.reshape(own, -1)
    piece = lax.all_gather(current, "orb", axis=0, tiled=True)
    flat = piece.reshape(piece.shape[0], -1)
    partial_rows = jnp.stack((cell_product(mine_y, flat), cell_product(mine_h, flat)))
    totals = lax.psum(partial_rows, "grid")
    correlation = totals[0] / cells
    hamiltonian = totals[1] / cells
    return (current, correlation, hamiltonian)


def solution(mesh):
    placed = (P("orb", "grid", None, None), P("grid", None, None))
    return jax.shard_map(
        per_device,
        mesh=mesh,
        in_specs=placed,
        out_specs=(P("orb", "grid", None, None), P("orb", None), P("orb", None)),
        check_vma=False,
    )
```

profile of v0, /device:TPU:2, one launch (start us, length us, event | category | flops | bytes accessed | tf_op | source)
XLA Modules:
  0.0 278.0 jit_solution(2201647198759797791)
XLA Ops:
  7.2 1.1 fusion.257
  8.4 1.7 collective-permute-start.1
  10.0 6.8 %collective-permute-start = (f32[4,4,32,128]{3,2,1,0:T(8,128)S(1)}, f32[4,4,32,128]{3,2,1,0:T(8,128)S(1)}, u32[]{:S(2)}, u32[]{:S(2)}) collective-permute-start(f32[4,4,32,128]{3,2,1,0:T(8,128)S(1)} %get-tuple-element.144), channel_id=1, source_target_pairs={{4,0},{8,4},{12,8},{16,12},{20,16},{24,20},{28,24},{32,28},{36,32}... | collective-permute-start | bytes 786440 | tf_op jit(solution)/shard_map/ppermute | solution.py:20
  16.8 1.4 fusion.272
  20.2 0.7 copy-done.3
  21.0 2.1 collective-permute-done.1
  23.2 2.6 broadcast_multiply_fusion
  28.1 6.2 %collective-permute-start.2 = (f32[4,4,32,128]{3,2,1,0:T(8,128)S(1)}, f32[4,4,32,128]{3,2,1,0:T(8,128)S(1)}, u32[]{:S(2)}, u32[]{:S(2)}) collective-permute-start(f32[4,4,32,128]{3,2,1,0:T(8,128)S(1)} %get-tuple-element.110), channel_id=1, source_target_pairs={{4,0},{8,4},{12,8},{16,12},{20,16},{24,20},{28,24},{32,28},{36,32}... | collective-permute-start | bytes 786440 | tf_op jit(solution)/shard_map/ppermute | solution.py:20
  34.5 5.4 %collective-permute-done.3 = f32[4,4,32,128]{3,2,1,0:T(8,128)S(1)} collective-permute-done((f32[4,4,32,128]{3,2,1,0:T(8,128)S(1)}, f32[4,4,32,128]{3,2,1,0:T(8,128)S(1)}, u32[]{:S(2)}, u32[]{:S(2)}) %collective-permute-start.3) | collective-permute-done | bytes 262176 | tf_op jit(solution)/shard_map/ppermute | solution.py:19
  39.8 2.6 multiply_subtract_fusion.2
  44.8 6.2 %collective-permute-start.4 = (f32[4,4,32,128]{3,2,1,0:T(8,128)S(1)}, f32[4,4,32,128]{3,2,1,0:T(8,128)S(1)}, u32[]{:S(2)}, u32[]{:S(2)}) collective-permute-start(f32[4,4,32,128]{3,2,1,0:T(8,128)S(1)} %get-tuple-element.76), channel_id=1, source_target_pairs={{4,0},{8,4},{12,8},{16,12},{20,16},{24,20},{28,24},{32,28},{36,32}... | collective-permute-start | bytes 786440 | tf_op jit(solution)/shard_map/ppermute | solution.py:20
  51.1 4.4 %collective-permute-done.5 = f32[4,4,32,128]{3,2,1,0:T(8,128)S(1)} collective-permute-done((f32[4,4,32,128]{3,2,1,0:T(8,128)S(1)}, f32[4,4,32,128]{3,2,1,0:T(8,128)S(1)}, u32[]{:S(2)}, u32[]{:S(2)}) %collective-permute-start.5) | collective-permute-done | bytes 262176 | tf_op jit(solution)/shard_map/ppermute | solution.py:19
  55.5 2.6 multiply_subtract_fusion.1
  60.4 6.2 %collective-permute-start.6 = (f32[4,4,32,128]{3,2,1,0:T(8,128)S(1)}, f32[4,4,32,128]{3,2,1,0:T(8,128)S(1)}, u32[]{:S(2)}, u32[]{:S(2)}) collective-permute-start(f32[4,4,32,128]{3,2,1,0:T(8,128)S(1)} %get-tuple-element.42), channel_id=1, source_target_pairs={{4,0},{8,4},{12,8},{16,12},{20,16},{24,20},{28,24},{32,28},{36,32}... | collective-permute-start | bytes 786440 | tf_op jit(solution)/shard_map/ppermute | solution.py:20
  66.8 4.2 %collective-permute-done.7 = f32[4,4,32,128]{3,2,1,0:T(8,128)S(1)} collective-permute-done((f32[4,4,32,128]{3,2,1,0:T(8,128)S(1)}, f32[4,4,32,128]{3,2,1,0:T(8,128)S(1)}, u32[]{:S(2)}, u32[]{:S(2)}) %collective-permute-start.7) | collective-permute-done | bytes 262176 | tf_op jit(solution)/shard_map/ppermute | solution.py:19
  71.0 3.3 %multiply_subtract_fusion = f32[4,8,32,128]{3,2,1,0:T(8,128)} fusion(f32[4,8,32,128]{3,2,1,0:T(8,128)S(1)} %multiply_subtract_fusion.2, f32[4,8,32,128]{3,2,1,0:T(8,128)S(1)} %multiply_subtract_fusion.1, f32[4,8,32,4]{3,2,1,0:T(8,128)S(1)} %get-tuple-element.73, f32[4,8,32,124]{3,2,1,0:T(8,128)S(1)} %get-tuple-element.75, ...), kind=kLoop, calls=%fused_computation.282 | loop fusion | flops 9043968 | bytes 10616832 | tf_op jit(solution)/shard_map/sub | solution.py:56
  74.3 1.1 fusion.205
  75.9 6.5 %collective-permute-start.8 = (f32[4,4,32,128]{3,2,1,0:T(8,128)S(1)}, f32[4,4,32,128]{3,2,1,0:T(8,128)S(1)}, u32[]{:S(2)}, u32[]{:S(2)}) collective-permute-start(f32[4,4,32,128]{3,2,1,0:T(8,128)S(1)} %get-tuple-element.40), channel_id=1, source_target_pairs={{4,0},{8,4},{12,8},{16,12},{20,16},{24,20},{28,24},{32,28},{36,32}... | collective-permute-start | bytes 786440 | tf_op jit(solution)/shard_map/ppermute | solution.py:20
  84.4 2.1 collective-permute-done.9
  86.5 2.5 fusion.24
  89.0 13.2 %all-gather.2.cloned.1.call-done = f32[16,8,32,128]{3,2,1,0:T(8,128)} async-done(((f32[4,8,32,128]{3,2,1,0:T(8,128)}), f32[16,8,32,128]{3,2,1,0:T(8,128)}) %all-gather.2.cloned.1.call-update) | async-done | bytes 2097168 | tf_op jit(solution)/shard_map/all_gather | solution.py:67
  102.2 5.6 %fusion.4 = f32[1,4,16]{2,1,0:T(4,128)S(1)} fusion(f32[16,8,32,128]{3,2,1,0:T(8,128)} %all-gather.2.cloned.1.call-done, f32[4,8,32,128]{3,2,1,0:T(8,128)S(1)} %copy-done), kind=kOutput, calls=%fused_computation.28 | convolution fusion | flops 25165824 | bytes 2621696 | tf_op jit(solution)/shard_map/dot_general | solution.py:43
  107.8 4.0 %fusion.7 = f32[1,4,16]{2,1,0:T(4,128)S(1)} fusion(f32[16,8,32,128]{3,2,1,0:T(8,128)S(1)} %copy-done.2, f32[4,8,32,128]{3,2,1,0:T(8,128)S(1)} %fusion.24), kind=kOutput, calls=%fused_computation.29 | convolution fusion | flops 25165824 | bytes 2621696 | tf_op jit(solution)/shard_map/dot_general | solution.py:43
  111.8 158.7 %psum.7 = f32[2,4,16]{2,1,0:T(4,128)S(1)} all-reduce(f32[2,4,16]{2,1,0:T(4,128)S(1)} %pad_maximum_fusion.8), channel_id=1, replica_groups=mesh['grid'=64,'orb'=4] {'grid'}, use_global_device_ids=true, to_apply=%region_0.1 | all-reduce | flops 128 | bytes 1024 | tf_op jit(solution)/shard_map/psum | solution.py:70
  (106 shorter events, 12.0 us)
Async XLA Ops:
  7.2 11.1 %copy-start.1 = (f32[4,8,32,128]{3,2,1,0:T(8,128)S(1)}, f32[4,8,32,128]{3,2,1,0:T(8,128)}, u32[]{:S(2)}) copy-start(f32[4,8,32,128]{3,2,1,0:T(8,128)} %param.2) | copy-start | bytes 1572868
  7.2 95.0 %all-gather.2.cloned.1.call-start = ((), (), s32[]{:S(2)}) async-start(), calls=%async_computation | async-start | bytes 2621440 | tf_op jit(solution)/shard_map/all_gather | solution.py:67
  8.4 14.7 %collective-permute-start.1 = (f32[4,4,32,128]{3,2,1,0:T(8,128)S(1)}, f32[4,4,32,128]{3,2,1,0:T(8,128)S(1)}, u32[]{:S(2)}, u32[]{:S(2)}) collective-permute-start(f32[4,4,32,128]{3,2,1,0:T(8,128)S(1)} %get-tuple-element.145), channel_id=1, source_target_pairs={{0,4},{4,8},{8,12},{12,16},{16,20},{20,24},{24,28},{28,32},{32,36}... | collective-permute-start | bytes 786440 | tf_op jit(solution)/shard_map/ppermute | solution.py:19
  10.0 13.2 %collective-permute-start = (f32[4,4,32,128]{3,2,1,0:T(8,128)S(1)}, f32[4,4,32,128]{3,2,1,0:T(8,128)S(1)}, u32[]{:S(2)}, u32[]{:S(2)}) collective-permute-start(f32[4,4,32,128]{3,2,1,0:T(8,128)S(1)} %get-tuple-element.144), channel_id=1, source_target_pairs={{4,0},{8,4},{12,8},{16,12},{20,16},{24,20},{28,24},{32,28},{36,32}... | collective-permute-start | bytes 786440 | tf_op jit(solution)/shard_map/ppermute | solution.py:20
  20.0 0.9 copy-start.3
  28.0 11.8 %collective-permute-start.3 = (f32[4,4,32,128]{3,2,1,0:T(8,128)S(1)}, f32[4,4,32,128]{3,2,1,0:T(8,128)S(1)}, u32[]{:S(2)}, u32[]{:S(2)}) collective-permute-start(f32[4,4,32,128]{3,2,1,0:T(8,128)S(1)} %get-tuple-element.111), channel_id=1, source_target_pairs={{0,4},{4,8},{8,12},{12,16},{16,20},{20,24},{24,28},{28,32},{32,36}... | collective-permute-start | bytes 786440 | tf_op jit(solution)/shard_map/ppermute | solution.py:19
  28.1 11.7 %collective-permute-start.2 = (f32[4,4,32,128]{3,2,1,0:T(8,128)S(1)}, f32[4,4,32,128]{3,2,1,0:T(8,128)S(1)}, u32[]{:S(2)}, u32[]{:S(2)}) collective-permute-start(f32[4,4,32,128]{3,2,1,0:T(8,128)S(1)} %get-tuple-element.110), channel_id=1, source_target_pairs={{4,0},{8,4},{12,8},{16,12},{20,16},{24,20},{28,24},{32,28},{36,32}... | collective-permute-start | bytes 786440 | tf_op jit(solution)/shard_map/ppermute | solution.py:20
  44.7 10.9 %collective-permute-start.5 = (f32[4,4,32,128]{3,2,1,0:T(8,128)S(1)}, f32[4,4,32,128]{3,2,1,0:T(8,128)S(1)}, u32[]{:S(2)}, u32[]{:S(2)}) collective-permute-start(f32[4,4,32,128]{3,2,1,0:T(8,128)S(1)} %get-tuple-element.77), channel_id=1, source_target_pairs={{0,4},{4,8},{8,12},{12,16},{16,20},{20,24},{24,28},{28,32},{32,36}... | collective-permute-start | bytes 786440 | tf_op jit(solution)/shard_map/ppermute | solution.py:19
  44.8 10.8 %collective-permute-start.4 = (f32[4,4,32,128]{3,2,1,0:T(8,128)S(1)}, f32[4,4,32,128]{3,2,1,0:T(8,128)S(1)}, u32[]{:S(2)}, u32[]{:S(2)}) collective-permute-start(f32[4,4,32,128]{3,2,1,0:T(8,128)S(1)} %get-tuple-element.76), channel_id=1, source_target_pairs={{4,0},{8,4},{12,8},{16,12},{20,16},{24,20},{28,24},{32,28},{36,32}... | collective-permute-start | bytes 786440 | tf_op jit(solution)/shard_map/ppermute | solution.py:20
  60.3 10.7 %collective-permute-start.7 = (f32[4,4,32,128]{3,2,1,0:T(8,128)S(1)}, f32[4,4,32,128]{3,2,1,0:T(8,128)S(1)}, u32[]{:S(2)}, u32[]{:S(2)}) collective-permute-start(f32[4,4,32,128]{3,2,1,0:T(8,128)S(1)} %get-tuple-element.43), channel_id=1, source_target_pairs={{0,4},{4,8},{8,12},{12,16},{16,20},{20,24},{24,28},{28,32},{32,36}... | collective-permute-start | bytes 786440 | tf_op jit(solution)/shard_map/ppermute | solution.py:19
  60.4 10.6 %collective-permute-start.6 = (f32[4,4,32,128]{3,2,1,0:T(8,128)S(1)}, f32[4,4,32,128]{3,2,1,0:T(8,128)S(1)}, u32[]{:S(2)}, u32[]{:S(2)}) collective-permute-start(f32[4,4,32,128]{3,2,1,0:T(8,128)S(1)} %get-tuple-element.42), channel_id=1, source_target_pairs={{4,0},{8,4},{12,8},{16,12},{20,16},{24,20},{28,24},{32,28},{36,32}... | collective-permute-start | bytes 786440 | tf_op jit(solution)/shard_map/ppermute | solution.py:20
  74.3 1.2 copy-start
  75.8 10.7 %collective-permute-start.9 = (f32[4,4,32,128]{3,2,1,0:T(8,128)S(1)}, f32[4,4,32,128]{3,2,1,0:T(8,128)S(1)}, u32[]{:S(2)}, u32[]{:S(2)}) collective-permute-start(f32[4,4,32,128]{3,2,1,0:T(8,128)S(1)} %get-tuple-element.41), channel_id=1, source_target_pairs={{0,4},{4,8},{8,12},{12,16},{16,20},{20,24},{24,28},{28,32},{32,36}... | collective-permute-start | bytes 786440 | tf_op jit(solution)/shard_map/ppermute | solution.py:19
  75.9 10.6 %collective-permute-start.8 = (f32[4,4,32,128]{3,2,1,0:T(8,128)S(1)}, f32[4,4,32,128]{3,2,1,0:T(8,128)S(1)}, u32[]{:S(2)}, u32[]{:S(2)}) collective-permute-start(f32[4,4,32,128]{3,2,1,0:T(8,128)S(1)} %get-tuple-element.40), channel_id=1, source_target_pairs={{4,0},{8,4},{12,8},{16,12},{20,16},{24,20},{28,24},{32,28},{36,32}... | collective-permute-start | bytes 786440 | tf_op jit(solution)/shard_map/ppermute | solution.py:20
  102.2 5.6 %copy-start.2 = (f32[16,8,32,128]{3,2,1,0:T(8,128)S(1)}, f32[16,8,32,128]{3,2,1,0:T(8,128)}, u32[]{:S(2)}) copy-start(f32[16,8,32,128]{3,2,1,0:T(8,128)} %all-gather.2.cloned.1.call-done) | copy-start | bytes 6291460
Sparse Core Ops, SparseCore 0:
  74.4 27.6 all-gather.1
where the time goes:
time: 278 us
  blocking collectives  159 us (57%)
  starting transfers between devices  34 us (12%)
  waiting for transfers between devices  31.4 us (11%)
  local copies, waits for them, and re-layouts  15.4 us (6%)
  between operations  14.5 us (5%)
  other arithmetic  14.2 us (5%)
  matrix products  9.63 us (3%)
    psum x1, blocking collectives, per_device(): totals = lax.psum(partial_rows, 'grid')  159 us
    ppermute x5, starting transfers between devices, padded_2(): after = lax.ppermute(first, axis, down)  32 us
    ppermute x5, waiting for transfers between devices, padded_2(): before = lax.ppermute(last, axis, up)  18.2 us
    all_gather x1, waiting for transfers between devices, per_device(): piece = lax.all_gather(current, 'orb', axis=0, tiled=True)  13.2 us
    slice x64, local copies, waits for them, and re-layouts, apply_ham(): jnp.roll(field, shift_by, axis_pos) + jnp.roll(field, -shift_by, axis_pos)  9.91 us
    dot_general x2, matrix products, cell_product(): lax.dot_general(left, right, (((1,), (1,)), ((), ())), precision=lax.Prec...  9.63 us
    sub x3, other arithmetic, per_device(): 2.0 * sigma_new / half * (apply_ham(current, potential) - centre * current)  8.52 us
  transfers between devices with their start and end apart: 11, of which 6 were waited for; matrix products, arithmetic and copies ran while one was open for 3% of the time, Pallas kernels for 0%

commit v1 on v0

v1 whole, which is shorter than its diff:
```python
import jax
import jax.numpy as jnp
from jax import lax
from jax.experimental import pallas as pl
from jax.experimental.pallas import tpu as pltpu
from jax.sharding import PartitionSpec as P

COEFS = (-205.0 / 72.0, 8.0 / 5.0, -1.0 / 5.0, 8.0 / 315.0, -1.0 / 560.0)
LOWER = -1.0
CUT = 4.0
UPPER = 10.0

HALF = (UPPER - CUT) / 2.0
CENTRE = (UPPER + CUT) / 2.0
SIGMA_1 = HALF / (LOWER - CENTRE)


def chebyshev_factors():
    factors = [(SIGMA_1 / HALF, 0.0)]
    sigma = SIGMA_1
    for _ in range(3):
        sigma_new = 1.0 / (2.0 / SIGMA_1 - sigma)
        factors.append((2.0 * sigma_new / HALF, sigma * sigma_new))
        sigma = sigma_new
    return factors


FACTORS = chebyshev_factors()
REACH = 4
OWN = 8
NY = 32
NZ = 128
MESH = pl.DeviceIdType.MESH


def stencil_layer(src, orb, at, v_ref, v_at, scale, shift):
    here = src[orb, at]
    total = (scale * v_ref[v_at] + scale * (-shift - 1.5 * COEFS[0])) * here
    for k in range(1, REACH + 1):
        ring = src[orb, at + k] + src[orb, at - k]
        ring += pltpu.roll(here, k, 0) + pltpu.roll(here, NY - k, 0)
        ring += pltpu.roll(here, k, 1) + pltpu.roll(here, NZ - k, 1)
        total += (-0.5 * scale * COEFS[k]) * ring
    return total


def kernel(orbitals, potential, filtered, corr, ham,
           p0, p1, p2, p3, p4, hy, v_ref, every, acc, rows_1, rows_2,
           in_sem, v_send, v_recv, a_send, a_recv, b_send, b_recv, c_send, c_recv,
           x_send, x_recv, out_sem, r1_send, r1_recv, r2_send, r2_recv):
    g = lax.axis_index("grid")
    o = lax.axis_index("orb")
    x_lo, z, y = g // 32, (g // 4) % 8, g % 4
    up = (lax.rem(g + 1, 64), o)
    down = (lax.rem(g + 63, 64), o)
    o_core = o + 1 - 2 * lax.rem(o, 2)
    o_far = lax.rem(o + 2, 4)
    core = (g, o_core)
    far = (g, o_far)

    def peer_1(d):
        return (lax.rem(x_lo + d // 4, 2) * 32 + z * 4 + lax.rem(y + d % 4, 4), o)

    def peer_2(d):
        return (x_lo * 32 + lax.rem(z + d, 8) * 4 + y, o)

    barrier = pltpu.get_barrier_semaphore()
    partners = [up, down, core, far] + [peer_1(d) for d in range(1, 8)] + [peer_2(d) for d in range(1, 8)]
    for partner in partners:
        pl.semaphore_signal(barrier, inc=1, device_id=partner, device_id_type=MESH)

    own_v = pltpu.make_async_copy(potential, v_ref.at[pl.ds(REACH, OWN)], in_sem.at[4])
    own_v.start()
    own_in = [pltpu.make_async_copy(orbitals.at[i], p0.at[i, pl.ds(OWN, OWN)], in_sem.at[i]) for i in range(4)]
    for copy in own_in:
        copy.start()

    pl.semaphore_wait(barrier, len(partners))

    def remote(src, dst, send, recv, device):
        return pltpu.make_async_remote_copy(
            src_ref=src, dst_ref=dst, send_sem=send, recv_sem=recv, device_id=device, device_id_type=MESH
        )

    v_copies = [
        remote(potential.at[pl.ds(OWN - REACH, REACH)], v_ref.at[pl.ds(0, REACH)], v_send.at[0], v_recv.at[0], up),
        remote(potential.at[pl.ds(0, REACH)], v_ref.at[pl.ds(REACH + OWN, REACH)], v_send.at[1], v_recv.at[1], down),
    ]
    a_copies = [
        [
            remote(orbitals.at[i], p0.at[i, pl.ds(0, OWN)], a_send.at[i, 0], a_recv.at[i, 0], up),
            remote(orbitals.at[i], p0.at[i, pl.ds(2 * OWN, OWN)], a_send.at[i, 1], a_recv.at[i, 1], down),
        ]
        for i in range(4)
    ]
    b_copies = [
        [
            remote(p2.at[i, pl.ds(OWN, OWN)], p2.at[i, pl.ds(0, OWN)], b_send.at[i, 0], b_recv.at[i, 0], up),
            remote(p2.at[i, pl.ds(OWN, OWN)], p2.at[i, pl.ds(2 * OWN, OWN)], b_send.at[i, 1], b_recv.at[i, 1], down),
        ]
        for i in range(4)
    ]
    c_copies = [
        [
            remote(p4.at[i, pl.ds(OWN, REACH)], p4.at[i, pl.ds(0, REACH)], c_send.at[i, 0], c_recv.at[i, 0], up),
            remote(p4.at[i, pl.ds(REACH, REACH)], p4.at[i, pl.ds(REACH + OWN, REACH)], c_send.at[i, 1], c_recv.at[i, 1], down),
        ]
        for i in range(4)
    ]
    x_copies = [
        [
            remote(every.at[o, i], every.at[o, i], x_send.at[i, 0], x_recv.at[i, 0], core),
            remote(every.at[o, i], every.at[o, i], x_send.at[i, 1], x_recv.at[i, 1], far),
            remote(every.at[o_far, i], every.at[o_far, i], x_send.at[i, 2], x_recv.at[i, 2], core),
        ]
        for i in range(4)
    ]
    out_copies = [pltpu.make_async_copy(every.at[o, i], filtered.at[i], out_sem.at[i]) for i in range(4)]

    def start(copies):
        for copy in copies:
            copy.start()

    def arrived(copies):
        for copy in copies:
            copy.wait_recv()

    def layers(count, body):
        def step(at, carry):
            body(at)
            return carry
        lax.fori_loop(0, count, step, 0, unroll=2)

    def unit_a(i):
        if i == 0:
            own_v.wait()
            arrived(v_copies)
        own_in[i].wait()
        arrived(a_copies[i])

        def first(at):
            p1[i, at] = stencil_layer(p0, i, at + REACH, v_ref, at, FACTORS[0][0], CENTRE)
        layers(2 * OWN, first)

        def second(at):
            p2[i, at + OWN] = stencil_layer(
                p1, i, at + REACH, v_ref, at + REACH, FACTORS[1][0], CENTRE
            ) - FACTORS[1][1] * p0[i, at + OWN]
        layers(OWN, second)
        start(b_copies[i])

    def unit_b(i):
        arrived(b_copies[i])

        def third(at):
            p3[i, at] = stencil_layer(
                p2, i, at + REACH, v_ref, at, FACTORS[2][0], CENTRE
            ) - FACTORS[2][1] * p1[i, at]
        layers(2 * OWN, third)

        def fourth(at):
            value = stencil_layer(
                p3, i, at + REACH, v_ref, at + REACH, FACTORS[3][0], CENTRE
            ) - FACTORS[3][1] * p2[i, at + OWN]
            p4[i, at + REACH] = value
            every[o, i, at] = value
        layers(OWN, fourth)
        start(c_copies[i])
        x_copies[i][1].start()
        x_copies[i][0].start()
        out_copies[i].start()

    def unit_c(i):
        arrived(c_copies[i])

        def applied(at):
            hy[i, at] = stencil_layer(p4, i, at + REACH, v_ref, at + REACH, 1.0, 0.0)
        layers(OWN, applied)
        x_copies[i][1].wait_recv()
        x_copies[i][2].start()

    def products(fields, partners_of):
        def step(at, sums):
            sums = list(sums)
            for part in range(NY // 8):
                rows = pl.ds(part * 8, 8)
                left = [hy[i, at, rows, :] if kind else every[o, i, at, rows, :] for kind, i in fields]
                for n, (slot, j) in enumerate(partners_of):
                    right = every[slot, j, at, rows, :]
                    for m in range(len(fields)):
                        sums[m * len(partners_of) + n] += left[m] * right
            return tuple(sums)

        zero = jnp.zeros((8, NZ), jnp.float32)
        sums = lax.fori_loop(0, OWN, step, (zero,) * (len(fields) * len(partners_of)))
        for m, (kind, i) in enumerate(fields):
            for n, (slot, j) in enumerate(partners_of):
                acc[(kind * 4 + i) * 16 + slot * 4 + j] = sums[m * len(partners_of) + n]

    def unit_d(i):
        x_copies[i][0].wait_recv()
        x_copies[i][2].wait_recv()
        products([(0, i), (1, i)], [(slot, j) for slot in range(4) for j in range(i + 1)])
        if i:
            products([(kind, m) for kind in range(2) for m in range(i)], [(slot, i) for slot in range(4)])

    start(v_copies)
    start(a_copies[0])
    start(a_copies[1])
    start(a_copies[2])
    unit_a(0)
    start(a_copies[3])
    unit_a(1)
    unit_a(2)
    unit_b(0)
    unit_a(3)
    unit_b(1)
    unit_c(0)
    unit_d(0)
    unit_b(2)
    unit_c(1)
    unit_d(1)
    unit_b(3)
    unit_c(2)
    unit_d(2)
    unit_c(3)
    unit_d(3)

    sums = jnp.sum(acc[...], axis=1)
    flat = lax.dot_general(
        jnp.full((8, NZ), 1.0 / (512 * NY * NZ), jnp.float32), sums, (((1,), (1,)), ((), ())),
        precision=lax.Precision.HIGHEST, preferred_element_type=jnp.float32,
    )
    row = lax.broadcasted_iota(jnp.int32, (8, NZ), 0)
    tile = flat
    for r in range(1, 8):
        tile = jnp.where(row == r, pltpu.roll(flat, NZ - 16 * r, 1), tile)

    me_1 = x_lo * 4 + y
    rows_1[me_1] = tile
    copies_1 = [remote(rows_1.at[me_1], rows_1.at[me_1], r1_send.at[d - 1], r1_recv.at[d - 1], peer_1(d)) for d in range(1, 8)]
    start(copies_1)
    arrived(copies_1)
    rows_2[z] = jnp.sum(rows_1[...], axis=0)
    copies_2 = [remote(rows_2.at[z], rows_2.at[z], r2_send.at[d - 1], r2_recv.at[d - 1], peer_2(d)) for d in range(1, 8)]
    start(copies_2)
    arrived(copies_2)
    tile = jnp.sum(rows_2[...], axis=0)
    corr[...] = tile[0:4, 0:16]
    ham[...] = tile[4:8, 0:16]

    for copies in [v_copies, copies_1, copies_2] + a_copies + b_copies + c_copies + x_copies:
        for copy in copies:
            copy.wait_send()
    for copy in out_copies:
        copy.wait()


def per_device(orbitals, potential):
    dma = pltpu.SemaphoreType.DMA
    field = lambda count: pltpu.VMEM((4, count, NY, NZ), jnp.float32)
    return pl.pallas_call(
        kernel,
        out_shape=(
            jax.ShapeDtypeStruct((4, OWN, NY, NZ), jnp.float32),
            jax.ShapeDtypeStruct((4, 16), jnp.float32),
            jax.ShapeDtypeStruct((4, 16), jnp.float32),
        ),
        in_specs=[pl.BlockSpec(memory_space=pl.ANY)] * 2,
        out_specs=(
            pl.BlockSpec(memory_space=pl.ANY),
            pl.BlockSpec(memory_space=pltpu.VMEM),
            pl.BlockSpec(memory_space=pltpu.VMEM),
        ),
        scratch_shapes=[
            field(3 * OWN), field(2 * OWN), field(3 * OWN), field(2 * OWN), field(2 * OWN), field(OWN),
            pltpu.VMEM((2 * OWN, NY, NZ), jnp.float32),
            pltpu.VMEM((4, 4, OWN, NY, NZ), jnp.float32),
            pltpu.VMEM((128, 8, NZ), jnp.float32),
            pltpu.VMEM((8, 8, NZ), jnp.float32),
            pltpu.VMEM((8, 8, NZ), jnp.float32),
            dma((5,)), dma((2,)), dma((2,)),
            dma((4, 2)), dma((4, 2)), dma((4, 2)), dma((4, 2)), dma((4, 2)), dma((4, 2)),
            dma((4, 3)), dma((4, 3)), dma((4,)),
            dma((7,)), dma((7,)), dma((7,)), dma((7,)),
        ],
        compiler_params=pltpu.CompilerParams(
            collective_id=0, has_side_effects=True, vmem_limit_bytes=40 * 1024 * 1024
        ),
    )(orbitals, potential)


def solution(mesh):
    return jax.shard_map(
        per_device,
        mesh=mesh,
        in_specs=(P("orb", "grid", None, None), P("grid", None, None)),
        out_specs=(P("orb", "grid", None, None), P("orb", None), P("orb", None)),
        check_vma=False,
    )
```

time: 278 us -> 69.9 us (0.25)
  blocking collectives: 159 us -> 0 us
  Pallas kernels: 0 us -> 65.2 us
  starting transfers between devices: 34 us -> 0 us
  waiting for transfers between devices: 31.4 us -> 0 us
  other arithmetic: 14.2 us -> 0 us
  between operations: 14.5 us -> 0.65 us
  local copies, waits for them, and re-layouts: 15.4 us -> 3.89 us
  matrix products: 9.63 us -> 0 us
    psum x1 -> x0, blocking collectives: 159 us -> none  [per_device(): totals = lax.psum(partial_rows, 'grid')]
    pallas_call x0 -> x1, Pallas kernels: none -> 65.2 us  [per_device(): pl.pallas_call(kernel, out_shape=(jax.ShapeDtypeStruct((4, OWN, NY, NZ),...]
    ppermute x10 -> x0, starting transfers between devices: 34 us -> none  [the longest x5 32 us: padded_2(): after = lax.ppermute(first, axis, down)]
    ppermute x10 -> x0, waiting for transfers between devices: 18.3 us -> none  [the longest x5 18.2 us: padded_2(): before = lax.ppermute(last, axis, up)]
    slice x85 -> x0, local copies, waits for them, and re-layouts: 14.4 us -> none  [the longest x64 9.91 us: apply_ham(): jnp.roll(field, shift_by, axis_pos) + jnp.roll(field, -shift_by, axis_pos)]
    all_gather x1 -> x0, waiting for transfers between devices: 13.2 us -> none  [per_device(): piece = lax.all_gather(current, 'orb', axis=0, tiled=True)]
    dot_general x2 -> x0, matrix products: 9.63 us -> none  [cell_product(): lax.dot_general(left, right, (((1,), (1,)), ((), ())), precision=lax.Prec...]
    sub x3 -> x0, other arithmetic: 8.52 us -> none  [per_device(): 2.0 * sigma_new / half * (apply_ham(current, potential) - centre * current)]
  transfers between devices with their start and end apart: 11 -> 0, of which waited for: 6 -> 0; matrix products, arithmetic and copies ran while one was open for 3% -> 0% of each run, Pallas kernels for 0% -> 0%
where the time goes in v1:
time: 69.9 us; the launch traced here: 69.7 us
  Pallas kernels  65.2 us (93%)
  local copies, waits for them, and re-layouts  3.89 us (6%)
    pallas_call x1, Pallas kernels, per_device(): pl.pallas_call(kernel, out_shape=(jax.ShapeDtypeStruct((4, OWN, NY, NZ),...  65.2 us
    unnamed x7, local copies, waits for them, and re-layouts  3.89 us

profile of v1, /device:TPU:2, one launch (start us, length us, event | category | flops | bytes accessed | tf_op | source)
XLA Modules:
  0.0 69.7 jit_solution(11948896590637593363)
XLA Ops:
  0.6 0.0 copy-start
  0.6 1.0 %copy-done = f32[4,8,32,128]{3,2,1,0:T(8,128)S(1)} copy-done((f32[4,8,32,128]{3,2,1,0:T(8,128)S(1)}, f32[4,8,32,128]{3,2,1,0:T(8,128)}, u32[]{:S(2)}) %copy-start) | copy-done | bytes 524312
  1.7 0.0 copy-start.1
  1.7 0.9 %copy-done.1 = f32[8,32,128]{2,1,0:T(8,128)S(1)} copy-done((f32[8,32,128]{2,1,0:T(8,128)S(1)}, f32[8,32,128]{2,1,0:T(8,128)}, u32[]{:S(2)}) %copy-start.1) | copy-done | bytes 131096
  2.6 65.2 %shard_map.49 = (f32[4,8,32,128]{3,2,1,0:T(8,128)S(1)}, f32[4,16]{1,0:T(4,128)S(1)}, f32[4,16]{1,0:T(4,128)S(1)}) custom-call(f32[4,8,32,128]{3,2,1,0:T(8,128)S(1)} %copy-done, f32[8,32,128]{2,1,0:T(8,128)S(1)} %copy-done.1), custom_call_target="tpu_custom_call" | custom-call | tf_op jit(solution)/shard_map/pallas_call | solution.py:262
  67.8 0.8 %copy.8 = f32[4,8,32,128]{3,2,1,0:T(8,128)} copy(f32[4,8,32,128]{3,2,1,0:T(8,128)S(1)} %get-tuple-element.6) | data formatting | bytes 1048576
  68.6 0.6 copy.9
  69.1 0.6 copy.10
Async XLA Ops:
  0.6 1.0 %copy-start = (f32[4,8,32,128]{3,2,1,0:T(8,128)S(1)}, f32[4,8,32,128]{3,2,1,0:T(8,128)}, u32[]{:S(2)}) copy-start(f32[4,8,32,128]{3,2,1,0:T(8,128)} %orbitals.1) | copy-start | bytes 1572868
  1.7 0.9 %copy-start.1 = (f32[8,32,128]{2,1,0:T(8,128)S(1)}, f32[8,32,128]{2,1,0:T(8,128)}, u32[]{:S(2)}) copy-start(f32[8,32,128]{2,1,0:T(8,128)} %potential.1) | copy-start | bytes 393220

commit v2 on v1

--- a/solution.py
+++ b/solution.py
@@ -33,21 +33,33 @@
 MESH = pl.DeviceIdType.MESH
 
 
+EVEN = (COEFS[2] + COEFS[4]) / 2.0
+ODD = (COEFS[4] - COEFS[2]) / 2.0
+
+
 def stencil_layer(src, orb, at, v_ref, v_at, scale, shift):
     here = src[orb, at]
+    factor = -0.5 * scale
+    near = src[orb, at + 1] + src[orb, at - 1]
+    third = (factor * COEFS[3]) * here
     total = (scale * v_ref[v_at] + scale * (-shift - 1.5 * COEFS[0])) * here
-    for k in range(1, REACH + 1):
-        ring = src[orb, at + k] + src[orb, at - k]
-        ring += pltpu.roll(here, k, 0) + pltpu.roll(here, NY - k, 0)
-        ring += pltpu.roll(here, k, 1) + pltpu.roll(here, NZ - k, 1)
-        total += (-0.5 * scale * COEFS[k]) * ring
+    for axis, size in ((1, NZ), (0, NY)):
+        after, before = pltpu.roll(here, 1, axis), pltpu.roll(here, size - 1, axis)
+        both = after + before
+        even = third + (factor * EVEN) * both
+        odd = (factor * ODD) * (after - before)
+        near += both
+        total += pltpu.roll(even + odd, 3, axis) + pltpu.roll(even - odd, size - 3, axis)
+    total += (factor * COEFS[1]) * near
+    for k in range(2, REACH + 1):
+        total += (factor * COEFS[k]) * (src[orb, at + k] + src[orb, at - k])
     return total
 
 
 def kernel(orbitals, potential, filtered, corr, ham,
-           p0, p1, p2, p3, p4, hy, v_ref, every, acc, rows_1, rows_2,
+           p0, p1, p2, p3, p4, hy, v_ref, every, acc, rows,
            in_sem, v_send, v_recv, a_send, a_recv, b_send, b_recv, c_send, c_recv,
-           x_send, x_recv, out_sem, r1_send, r1_recv, r2_send, r2_recv):
+           x_send, x_recv, out_sem, r_send, r_recv):
     g = lax.axis_index("grid")
     o = lax.axis_index("orb")
     x_lo, z, y = g // 32, (g // 4) % 8, g % 4
@@ -57,15 +69,23 @@
     o_far = lax.rem(o + 2, 4)
     core = (g, o_core)
     far = (g, o_far)
-
-    def peer_1(d):
-        return (lax.rem(x_lo + d // 4, 2) * 32 + z * 4 + lax.rem(y + d % 4, 4), o)
-
-    def peer_2(d):
-        return (x_lo * 32 + lax.rem(z + d, 8) * 4 + y, o)
+    corner_up = (z == 7) & (y == 3) & (lax.rem(o, 2) == 1)
+    corner_down = (z == 0) & (y == 0) & (lax.rem(o, 2) == 1)
+    corner = corner_up | corner_down
+    across = (lax.rem(g + 32, 64), o)
+    onward = (x_lo * 32 + jnp.where(corner_up, 0, 31), o)
+    up_first = (jnp.where(corner_up, across[0], up[0]), o)
+    down_first = (jnp.where(corner_down, across[0], down[0]), o)
+    up_at, up_sem = jnp.where(corner_up, 3 * OWN, 0), jnp.where(corner_up, 2, 0)
+    down_at, down_sem = jnp.where(corner_down, 3 * OWN, 2 * OWN), jnp.where(corner_down, 2, 1)
+    onward_at, onward_sem = jnp.where(corner_up, 0, 2 * OWN), jnp.where(corner_up, 0, 1)
+
+    offsets = [(dx, dz, dy) for dx in range(2) for dz in range(8) for dy in range(4) if dx or dz or dy]
+    offsets.sort(key=lambda d: -(d[0] + min(d[1], 8 - d[1]) + min(d[2], 4 - d[2])))
+    others = [(lax.rem(x_lo + dx, 2) * 32 + lax.rem(z + dz, 8) * 4 + lax.rem(y + dy, 4), o) for dx, dz, dy in offsets]
 
     barrier = pltpu.get_barrier_semaphore()
-    partners = [up, down, core, far] + [peer_1(d) for d in range(1, 8)] + [peer_2(d) for d in range(1, 8)]
+    partners = others + [core, far]
     for partner in partners:
         pl.semaphore_signal(barrier, inc=1, device_id=partner, device_id_type=MESH)
 
@@ -86,20 +106,37 @@
         remote(potential.at[pl.ds(OWN - REACH, REACH)], v_ref.at[pl.ds(0, REACH)], v_send.at[0], v_recv.at[0], up),
         remote(potential.at[pl.ds(0, REACH)], v_ref.at[pl.ds(REACH + OWN, REACH)], v_send.at[1], v_recv.at[1], down),
     ]
-    a_copies = [
-        [
-            remote(orbitals.at[i], p0.at[i, pl.ds(0, OWN)], a_send.at[i, 0], a_recv.at[i, 0], up),
-            remote(orbitals.at[i], p0.at[i, pl.ds(2 * OWN, OWN)], a_send.at[i, 1], a_recv.at[i, 1], down),
+
+    def block_copies(i, src, dst, send, recv):
+        return [
+            remote(src, dst.at[i, pl.ds(up_at, OWN)], send.at[i, 0], recv.at[i, up_sem], up_first),
+            remote(src, dst.at[i, pl.ds(down_at, OWN)], send.at[i, 1], recv.at[i, down_sem], down_first),
         ]
-        for i in range(4)
-    ]
-    b_copies = [
-        [
-            remote(p2.at[i, pl.ds(OWN, OWN)], p2.at[i, pl.ds(0, OWN)], b_send.at[i, 0], b_recv.at[i, 0], up),
-            remote(p2.at[i, pl.ds(OWN, OWN)], p2.at[i, pl.ds(2 * OWN, OWN)], b_send.at[i, 1], b_recv.at[i, 1], down),
+
+    def block_arrivals(i, dst, send, recv):
+        return [
+            remote(dst.at[i, pl.ds(0, OWN)], dst.at[i, pl.ds(0, OWN)], send.at[i, 0], recv.at[i, 0], up),
+            remote(dst.at[i, pl.ds(2 * OWN, OWN)], dst.at[i, pl.ds(2 * OWN, OWN)], send.at[i, 1], recv.at[i, 1], down),
         ]
-        for i in range(4)
-    ]
+
+    def corner_copy(i, dst, send, recv):
+        return remote(
+            dst.at[i, pl.ds(3 * OWN, OWN)], dst.at[i, pl.ds(onward_at, OWN)],
+            send.at[i, 2], recv.at[i, onward_sem], onward,
+        )
+
+    def send_onward(i, dst, send, recv):
+        @pl.when(corner)
+        def _():
+            remote(
+                dst.at[i, pl.ds(3 * OWN, OWN)], dst.at[i, pl.ds(3 * OWN, OWN)], send.at[i, 2], recv.at[i, 2], across
+            ).wait_recv()
+            corner_copy(i, dst, send, recv).start()
+
+    a_copies = [block_copies(i, orbitals.at[i], p0, a_send, a_recv) for i in range(4)]
+    a_arrivals = [block_arrivals(i, p0, a_send, a_recv) for i in range(4)]
+    b_copies = [block_copies(i, p2.at[i, pl.ds(OWN, OWN)], p2, b_send, b_recv) for i in range(4)]
+    b_arrivals = [block_arrivals(i, p2, b_send, b_recv) for i in range(4)]
     c_copies = [
         [
             remote(p4.at[i, pl.ds(OWN, REACH)], p4.at[i, pl.ds(0, REACH)], c_send.at[i, 0], c_recv.at[i, 0], up),
@@ -125,18 +162,25 @@
         for copy in copies:
             copy.wait_recv()
 
+    gone = []
+
+    def sent(copies):
+        for copy in copies:
+            copy.wait_send()
+        gone.append(copies)
+
     def layers(count, body):
         def step(at, carry):
             body(at)
             return carry
-        lax.fori_loop(0, count, step, 0, unroll=2)
+        lax.fori_loop(0, count, step, 0, unroll=8)
 
     def unit_a(i):
         if i == 0:
             own_v.wait()
             arrived(v_copies)
         own_in[i].wait()
-        arrived(a_copies[i])
+        arrived(a_arrivals[i])
 
         def first(at):
             p1[i, at] = stencil_layer(p0, i, at + REACH, v_ref, at, FACTORS[0][0], CENTRE)
@@ -147,10 +191,9 @@
                 p1, i, at + REACH, v_ref, at + REACH, FACTORS[1][0], CENTRE
             ) - FACTORS[1][1] * p0[i, at + OWN]
         layers(OWN, second)
-        start(b_copies[i])
 
     def unit_b(i):
-        arrived(b_copies[i])
+        arrived(b_arrivals[i])
 
         def third(at):
             p3[i, at] = stencil_layer(
@@ -165,7 +208,6 @@
             p4[i, at + REACH] = value
             every[o, i, at] = value
         layers(OWN, fourth)
-        start(c_copies[i])
         x_copies[i][1].start()
         x_copies[i][0].start()
         out_copies[i].start()
@@ -204,24 +246,40 @@
         if i:
             products([(kind, m) for kind in range(2) for m in range(i)], [(slot, i) for slot in range(4)])
 
+    start(a_copies[0])
     start(v_copies)
-    start(a_copies[0])
     start(a_copies[1])
     start(a_copies[2])
+    start(a_copies[3])
+    send_onward(0, p0, a_send, a_recv)
+    send_onward(1, p0, a_send, a_recv)
+    send_onward(2, p0, a_send, a_recv)
+    send_onward(3, p0, a_send, a_recv)
     unit_a(0)
-    start(a_copies[3])
+    start(b_copies[0])
     unit_a(1)
+    start(b_copies[1])
+    send_onward(0, p2, b_send, b_recv)
     unit_a(2)
+    start(b_copies[2])
+    send_onward(1, p2, b_send, b_recv)
+    unit_a(3)
+    start(b_copies[3])
+    send_onward(2, p2, b_send, b_recv)
     unit_b(0)
-    unit_a(3)
+    start(c_copies[0])
+    send_onward(3, p2, b_send, b_recv)
     unit_b(1)
+    start(c_copies[1])
+    unit_b(2)
+    start(c_copies[2])
+    unit_b(3)
+    start(c_copies[3])
     unit_c(0)
+    unit_c(1)
+    unit_c(2)
     unit_d(0)
-    unit_b(2)
-    unit_c(1)
     unit_d(1)
-    unit_b(3)
-    unit_c(2)
     unit_d(2)
     unit_c(3)
     unit_d(3)
@@ -231,29 +289,30 @@
         jnp.full((8, NZ), 1.0 / (512 * NY * NZ), jnp.float32), sums, (((1,), (1,)), ((), ())),
         precision=lax.Precision.HIGHEST, preferred_element_type=jnp.float32,
     )
-    row = lax.broadcasted_iota(jnp.int32, (8, NZ), 0)
-    tile = flat
-    for r in range(1, 8):
-        tile = jnp.where(row == r, pltpu.roll(flat, NZ - 16 * r, 1), tile)
-
-    me_1 = x_lo * 4 + y
-    rows_1[me_1] = tile
-    copies_1 = [remote(rows_1.at[me_1], rows_1.at[me_1], r1_send.at[d - 1], r1_recv.at[d - 1], peer_1(d)) for d in range(1, 8)]
-    start(copies_1)
-    arrived(copies_1)
-    rows_2[z] = jnp.sum(rows_1[...], axis=0)
-    copies_2 = [remote(rows_2.at[z], rows_2.at[z], r2_send.at[d - 1], r2_recv.at[d - 1], peer_2(d)) for d in range(1, 8)]
-    start(copies_2)
-    arrived(copies_2)
-    tile = jnp.sum(rows_2[...], axis=0)
-    corr[...] = tile[0:4, 0:16]
-    ham[...] = tile[4:8, 0:16]
-
-    for copies in [v_copies, copies_1, copies_2] + a_copies + b_copies + c_copies + x_copies:
-        for copy in copies:
-            copy.wait_send()
+    rows[pl.ds(g, 1)] = flat[0:1]
+    sum_copies = [
+        remote(rows.at[pl.ds(g, 1)], rows.at[pl.ds(g, 1)], r_send.at[n], r_recv.at[n], peer)
+        for n, peer in enumerate(others)
+    ]
+    start(sum_copies)
+    arrived(sum_copies)
+    total = jnp.sum(rows[...], axis=0, keepdims=True)
+    for kind, ref in ((0, corr), (1, ham)):
+        for i in range(4):
+            first = (kind * 4 + i) * 16
+            ref[pl.ds(i, 1), :] = total[:, first : first + 16]
+
+    for copies in [v_copies, sum_copies] + a_copies + b_copies + c_copies + x_copies:
+        if not any(copies is other for other in gone):
+            sent(copies)
     for copy in out_copies:
         copy.wait()
+
+    @pl.when(corner)
+    def _():
+        for i in range(4):
+            corner_copy(i, p0, a_send, a_recv).wait_send()
+            corner_copy(i, p2, b_send, b_recv).wait_send()
 
 
 def per_device(orbitals, potential):
@@ -273,19 +332,18 @@
             pl.BlockSpec(memory_space=pltpu.VMEM),
         ),
         scratch_shapes=[
-            field(3 * OWN), field(2 * OWN), field(3 * OWN), field(2 * OWN), field(2 * OWN), field(OWN),
+            field(4 * OWN), field(2 * OWN), field(4 * OWN), field(2 * OWN), field(2 * OWN), field(OWN),
             pltpu.VMEM((2 * OWN, NY, NZ), jnp.float32),
             pltpu.VMEM((4, 4, OWN, NY, NZ), jnp.float32),
             pltpu.VMEM((128, 8, NZ), jnp.float32),
-            pltpu.VMEM((8, 8, NZ), jnp.float32),
-            pltpu.VMEM((8, 8, NZ), jnp.float32),
+            pltpu.VMEM((64, NZ), jnp.float32),
             dma((5,)), dma((2,)), dma((2,)),
-            dma((4, 2)), dma((4, 2)), dma((4, 2)), dma((4, 2)), dma((4, 2)), dma((4, 2)),
+            dma((4, 3)), dma((4, 3)), dma((4, 3)), dma((4, 3)), dma((4, 2)), dma((4, 2)),
             dma((4, 3)), dma((4, 3)), dma((4,)),
-            dma((7,)), dma((7,)), dma((7,)), dma((7,)),
+            dma((63,)), dma((63,)),
         ],
         compiler_params=pltpu.CompilerParams(
-            collective_id=0, has_side_effects=True, vmem_limit_bytes=40 * 1024 * 1024
+            collective_id=0, has_side_effects=True, vmem_limit_bytes=63 * 1024 * 1024
         ),
     )(orbitals, potential)
 

time: 69.9 us -> 64 us (0.916)
  Pallas kernels: 65.2 us -> 60 us
  local copies, waits for them, and re-layouts: 3.89 us -> 3.14 us
    pallas_call x1, Pallas kernels: 65.2 us -> 60 us  [per_device(): pl.pallas_call(kernel, out_shape=(jax.ShapeDtypeStruct((4, OWN, NY, NZ),...]
    unnamed x7, local copies, waits for them, and re-layouts: 3.89 us -> 3.14 us
where the time goes in v2:
time: 64 us; the launch traced here: 63.8 us
  Pallas kernels  60 us (94%)
  local copies, waits for them, and re-layouts  3.14 us (5%)
  between operations  0.65 us (1%)
    pallas_call x1, Pallas kernels, per_device(): pl.pallas_call(kernel, out_shape=(jax.ShapeDtypeStruct((4, OWN, NY, NZ),...  60 us
    unnamed x7, local copies, waits for them, and re-layouts  3.14 us

profile of v2, /device:TPU:2, one launch (start us, length us, event | category | flops | bytes accessed | tf_op | source)
XLA Modules:
  0.0 63.8 jit_solution(6708216703381595551)
XLA Ops:
  0.6 60.0 %shard_map.49 = (f32[4,8,32,128]{3,2,1,0:T(8,128)}, f32[4,16]{1,0:T(4,128)}, f32[4,16]{1,0:T(4,128)}) custom-call(f32[4,8,32,128]{3,2,1,0:T(8,128)} %orbitals.1, f32[8,32,128]{2,1,0:T(8,128)} %potential.1), custom_call_target="tpu_custom_call" | custom-call | tf_op jit(solution)/shard_map/pallas_call | solution.py:321
  60.7 0.0 copy-start.1
  60.7 1.9 %copy.8 = f32[4,8,32,128]{3,2,1,0:T(8,128)} copy(f32[4,8,32,128]{3,2,1,0:T(8,128)} %get-tuple-element.6) | data formatting | bytes 1048576
  62.6 0.0 copy-done.1
  62.6 0.0 copy-start
  62.6 0.6 copy.9
  63.1 0.1 copy-done
  63.2 0.6 copy.10
Async XLA Ops:
  60.7 1.9 %copy-start.1 = (f32[4,16]{1,0:T(4,128)S(1)}, f32[4,16]{1,0:T(4,128)}, u32[]{:S(2)}) copy-start(f32[4,16]{1,0:T(4,128)} %get-tuple-element.7) | copy-start | bytes 772
  62.6 0.7 %copy-start = (f32[4,16]{1,0:T(4,128)S(1)}, f32[4,16]{1,0:T(4,128)}, u32[]{:S(2)}) copy-start(f32[4,16]{1,0:T(4,128)} %get-tuple-element.8) | copy-start | bytes 772

commit v3 on v2

--- a/solution.py
+++ b/solution.py
@@ -59,7 +59,7 @@
 def kernel(orbitals, potential, filtered, corr, ham,
            p0, p1, p2, p3, p4, hy, v_ref, every, acc, rows,
            in_sem, v_send, v_recv, a_send, a_recv, b_send, b_recv, c_send, c_recv,
-           x_send, x_recv, out_sem, r_send, r_recv):
+           x_send, x_recv, out_sem, r_send, r_recv, met):
     g = lax.axis_index("grid")
     o = lax.axis_index("orb")
     x_lo, z, y = g // 32, (g // 4) % 8, g % 4
@@ -85,9 +85,22 @@
     others = [(lax.rem(x_lo + dx, 2) * 32 + lax.rem(z + dz, 8) * 4 + lax.rem(y + dy, 4), o) for dx, dz, dy in offsets]
 
     barrier = pltpu.get_barrier_semaphore()
-    partners = others + [core, far]
+    beside = [(x_lo * 32 + lax.rem(z + d, 8) * 4 + y, o) for d in (1, 7)]
+    partners = [up, down, across] + beside + [core, far]
     for partner in partners:
         pl.semaphore_signal(barrier, inc=1, device_id=partner, device_id_type=MESH)
+
+    def along_z(d):
+        return (x_lo * 32 + lax.rem(z + d, 8) * 4 + y, o)
+
+    rounds = [beside, [along_z(2), along_z(6)], [along_z(4)], [up, down], [across]]
+
+    def greet(n):
+        for partner in rounds[n]:
+            pl.semaphore_signal(met.at[n], inc=1, device_id=partner, device_id_type=MESH)
+
+    def heard(n):
+        pl.semaphore_wait(met.at[n], len(rounds[n]))
 
     own_v = pltpu.make_async_copy(potential, v_ref.at[pl.ds(REACH, OWN)], in_sem.at[4])
     own_v.start()
@@ -102,9 +115,17 @@
             src_ref=src, dst_ref=dst, send_sem=send, recv_sem=recv, device_id=device, device_id_type=MESH
         )
 
+    half = REACH // 2
+    part = half * lax.rem(o, 2)
+    above = v_ref.at[pl.ds(part, half)]
+    below = v_ref.at[pl.ds(REACH + OWN + part, half)]
     v_copies = [
-        remote(potential.at[pl.ds(OWN - REACH, REACH)], v_ref.at[pl.ds(0, REACH)], v_send.at[0], v_recv.at[0], up),
-        remote(potential.at[pl.ds(0, REACH)], v_ref.at[pl.ds(REACH + OWN, REACH)], v_send.at[1], v_recv.at[1], down),
+        remote(potential.at[pl.ds(OWN - REACH + part, half)], above, v_send.at[0], v_recv.at[0], up),
+        remote(potential.at[pl.ds(part, half)], below, v_send.at[1], v_recv.at[1], down),
+    ]
+    v_shared = [
+        remote(above, above, v_send.at[2], v_recv.at[2], core),
+        remote(below, below, v_send.at[3], v_recv.at[3], core),
     ]
 
     def block_copies(i, src, dst, send, recv):
@@ -179,8 +200,11 @@
         if i == 0:
             own_v.wait()
             arrived(v_copies)
+            start(v_shared)
         own_in[i].wait()
         arrived(a_arrivals[i])
+        if i == 0:
+            arrived(v_shared)
 
         def first(at):
             p1[i, at] = stencil_layer(p0, i, at + REACH, v_ref, at, FACTORS[0][0], CENTRE)
@@ -218,6 +242,8 @@
         def applied(at):
             hy[i, at] = stencil_layer(p4, i, at + REACH, v_ref, at + REACH, 1.0, 0.0)
         layers(OWN, applied)
+
+    def pass_on(i):
         x_copies[i][1].wait_recv()
         x_copies[i][2].start()
 
@@ -237,35 +263,51 @@
         sums = lax.fori_loop(0, OWN, step, (zero,) * (len(fields) * len(partners_of)))
         for m, (kind, i) in enumerate(fields):
             for n, (slot, j) in enumerate(partners_of):
-                acc[(kind * 4 + i) * 16 + slot * 4 + j] = sums[m * len(partners_of) + n]
-
-    def unit_d(i):
+                value = jnp.sum(sums[m * len(partners_of) + n], axis=0, keepdims=True)
+                acc[pl.ds((kind * 4 + i) * 16 + slot * 4 + j, 1), :] = value
+
+    def unit_d(i, slots):
+        products([(0, i), (1, i)], [(slot, j) for slot in slots for j in range(i + 1)])
+        if i:
+            products([(kind, m) for kind in range(2) for m in range(i)], [(slot, i) for slot in slots])
+
+    def unit_n(i):
         x_copies[i][0].wait_recv()
+        unit_d(i, (o, o_core))
+
+    def unit_f(i):
         x_copies[i][2].wait_recv()
-        products([(0, i), (1, i)], [(slot, j) for slot in range(4) for j in range(i + 1)])
-        if i:
-            products([(kind, m) for kind in range(2) for m in range(i)], [(slot, i) for slot in range(4)])
+        unit_d(i, (o_far, lax.rem(o_core + 2, 4)))
 
     start(a_copies[0])
     start(v_copies)
+    greet(0)
     start(a_copies[1])
     start(a_copies[2])
     start(a_copies[3])
     send_onward(0, p0, a_send, a_recv)
     send_onward(1, p0, a_send, a_recv)
+    heard(0)
+    greet(1)
     send_onward(2, p0, a_send, a_recv)
     send_onward(3, p0, a_send, a_recv)
     unit_a(0)
     start(b_copies[0])
+    heard(1)
+    greet(2)
     unit_a(1)
     start(b_copies[1])
     send_onward(0, p2, b_send, b_recv)
+    heard(2)
+    greet(3)
     unit_a(2)
     start(b_copies[2])
     send_onward(1, p2, b_send, b_recv)
     unit_a(3)
     start(b_copies[3])
     send_onward(2, p2, b_send, b_recv)
+    heard(3)
+    greet(4)
     unit_b(0)
     start(c_copies[0])
     send_onward(3, p2, b_send, b_recv)
@@ -273,20 +315,28 @@
     start(c_copies[1])
     unit_b(2)
     start(c_copies[2])
+    heard(4)
     unit_b(3)
     start(c_copies[3])
     unit_c(0)
+    pass_on(0)
     unit_c(1)
+    pass_on(1)
+    unit_n(0)
+    unit_n(1)
     unit_c(2)
-    unit_d(0)
-    unit_d(1)
-    unit_d(2)
+    pass_on(2)
+    unit_n(2)
+    unit_f(0)
+    unit_f(1)
+    unit_f(2)
     unit_c(3)
-    unit_d(3)
-
-    sums = jnp.sum(acc[...], axis=1)
+    pass_on(3)
+    unit_n(3)
+    unit_f(3)
+
     flat = lax.dot_general(
-        jnp.full((8, NZ), 1.0 / (512 * NY * NZ), jnp.float32), sums, (((1,), (1,)), ((), ())),
+        jnp.full((8, NZ), 1.0 / (512 * NY * NZ), jnp.float32), acc[...], (((1,), (1,)), ((), ())),
         precision=lax.Precision.HIGHEST, preferred_element_type=jnp.float32,
     )
     rows[pl.ds(g, 1)] = flat[0:1]
@@ -302,7 +352,7 @@
             first = (kind * 4 + i) * 16
             ref[pl.ds(i, 1), :] = total[:, first : first + 16]
 
-    for copies in [v_copies, sum_copies] + a_copies + b_copies + c_copies + x_copies:
+    for copies in [v_copies, v_shared, sum_copies] + a_copies + b_copies + c_copies + x_copies:
         if not any(copies is other for other in gone):
             sent(copies)
     for copy in out_copies:
@@ -325,7 +375,7 @@
             jax.ShapeDtypeStruct((4, 16), jnp.float32),
             jax.ShapeDtypeStruct((4, 16), jnp.float32),
         ),
-        in_specs=[pl.BlockSpec(memory_space=pl.ANY)] * 2,
+        in_specs=[pl.BlockSpec(memory_space=pltpu.HBM)] * 2,
         out_specs=(
             pl.BlockSpec(memory_space=pl.ANY),
             pl.BlockSpec(memory_space=pltpu.VMEM),
@@ -335,15 +385,15 @@
             field(4 * OWN), field(2 * OWN), field(4 * OWN), field(2 * OWN), field(2 * OWN), field(OWN),
             pltpu.VMEM((2 * OWN, NY, NZ), jnp.float32),
             pltpu.VMEM((4, 4, OWN, NY, NZ), jnp.float32),
-            pltpu.VMEM((128, 8, NZ), jnp.float32),
+            pltpu.VMEM((128, NZ), jnp.float32),
             pltpu.VMEM((64, NZ), jnp.float32),
-            dma((5,)), dma((2,)), dma((2,)),
+            dma((5,)), dma((4,)), dma((4,)),
             dma((4, 3)), dma((4, 3)), dma((4, 3)), dma((4, 3)), dma((4, 2)), dma((4, 2)),
             dma((4, 3)), dma((4, 3)), dma((4,)),
-            dma((63,)), dma((63,)),
+            dma((63,)), dma((63,)), pltpu.SemaphoreType.REGULAR((5,)),
         ],
         compiler_params=pltpu.CompilerParams(
-            collective_id=0, has_side_effects=True, vmem_limit_bytes=63 * 1024 * 1024
+            collective_id=0, has_side_effects=True, vmem_limit_bytes=40 * 1024 * 1024
         ),
     )(orbitals, potential)
 

time: 64 us -> 61.4 us (0.959)
  Pallas kernels: 60 us -> 56.5 us
  local copies, waits for them, and re-layouts: 3.14 us -> 3.89 us
    pallas_call x1, Pallas kernels: 60 us -> 56.5 us  [per_device(): pl.pallas_call(kernel, out_shape=(jax.ShapeDtypeStruct((4, OWN, NY, NZ),...]
    unnamed x7, local copies, waits for them, and re-layouts: 3.14 us -> 3.89 us
where the time goes in v3:
time: 61.4 us; the launch traced here: 61 us
  Pallas kernels  56.5 us (92%)
  local copies, waits for them, and re-layouts  3.89 us (6%)
  between operations  0.65 us (1%)
    pallas_call x1, Pallas kernels, per_device(): pl.pallas_call(kernel, out_shape=(jax.ShapeDtypeStruct((4, OWN, NY, NZ),...  56.5 us
    unnamed x7, local copies, waits for them, and re-layouts  3.89 us

profile of v3, /device:TPU:2, one launch (start us, length us, event | category | flops | bytes accessed | tf_op | source)
XLA Modules:
  0.0 61.0 jit_solution(14117989952215057720)
XLA Ops:
  0.6 0.0 copy-start
  0.6 1.0 %copy-done = f32[4,8,32,128]{3,2,1,0:T(8,128)S(1)} copy-done((f32[4,8,32,128]{3,2,1,0:T(8,128)S(1)}, f32[4,8,32,128]{3,2,1,0:T(8,128)}, u32[]{:S(2)}) %copy-start) | copy-done | bytes 524312
  1.7 0.0 copy-start.1
  1.7 0.9 %copy-done.1 = f32[8,32,128]{2,1,0:T(8,128)S(1)} copy-done((f32[8,32,128]{2,1,0:T(8,128)S(1)}, f32[8,32,128]{2,1,0:T(8,128)}, u32[]{:S(2)}) %copy-start.1) | copy-done | bytes 131096
  2.6 56.5 %shard_map.49 = (f32[4,8,32,128]{3,2,1,0:T(8,128)S(1)}, f32[4,16]{1,0:T(4,128)S(1)}, f32[4,16]{1,0:T(4,128)S(1)}) custom-call(f32[4,8,32,128]{3,2,1,0:T(8,128)S(1)} %copy-done, f32[8,32,128]{2,1,0:T(8,128)S(1)} %copy-done.1), custom_call_target="tpu_custom_call" | custom-call | tf_op jit(solution)/shard_map/pallas_call | solution.py:371
  59.1 0.8 %copy.8 = f32[4,8,32,128]{3,2,1,0:T(8,128)} copy(f32[4,8,32,128]{3,2,1,0:T(8,128)S(1)} %get-tuple-element.6) | data formatting | bytes 1048576
  59.9 0.6 copy.9
  60.4 0.6 copy.10
Async XLA Ops:
  0.6 1.0 %copy-start = (f32[4,8,32,128]{3,2,1,0:T(8,128)S(1)}, f32[4,8,32,128]{3,2,1,0:T(8,128)}, u32[]{:S(2)}) copy-start(f32[4,8,32,128]{3,2,1,0:T(8,128)} %orbitals.1) | copy-start | bytes 1572868
  1.7 0.9 %copy-start.1 = (f32[8,32,128]{2,1,0:T(8,128)S(1)}, f32[8,32,128]{2,1,0:T(8,128)}, u32[]{:S(2)}) copy-start(f32[8,32,128]{2,1,0:T(8,128)} %potential.1) | copy-start | bytes 393220

commit v4 on v3

--- a/solution.py
+++ b/solution.py
@@ -286,13 +286,13 @@
     start(a_copies[2])
     start(a_copies[3])
     send_onward(0, p0, a_send, a_recv)
-    send_onward(1, p0, a_send, a_recv)
     heard(0)
     greet(1)
+    send_onward(1, p0, a_send, a_recv)
+    unit_a(0)
+    start(b_copies[0])
     send_onward(2, p0, a_send, a_recv)
     send_onward(3, p0, a_send, a_recv)
-    unit_a(0)
-    start(b_copies[0])
     heard(1)
     greet(2)
     unit_a(1)
@@ -308,9 +308,9 @@
     send_onward(2, p2, b_send, b_recv)
     heard(3)
     greet(4)
+    send_onward(3, p2, b_send, b_recv)
     unit_b(0)
     start(c_copies[0])
-    send_onward(3, p2, b_send, b_recv)
     unit_b(1)
     start(c_copies[1])
     unit_b(2)
@@ -366,6 +366,7 @@
 
 
 def per_device(orbitals, potential):
+    orbitals, potential = (pltpu.with_memory_space_constraint(value, pltpu.HBM) for value in (orbitals, potential))
     dma = pltpu.SemaphoreType.DMA
     field = lambda count: pltpu.VMEM((4, count, NY, NZ), jnp.float32)
     return pl.pallas_call(

time: 61.4 us -> 59.7 us (0.972)
  local copies, waits for them, and re-layouts: 3.89 us -> 1.95 us
    unnamed x7 -> x3, local copies, waits for them, and re-layouts: 3.89 us -> 1.95 us
where the time goes in v4:
time: 59.7 us; the launch traced here: 59.3 us
  Pallas kernels  56.7 us (95%)
  local copies, waits for them, and re-layouts  1.95 us (3%)
  between operations  0.64 us (1%)
    pallas_call x1, Pallas kernels, per_device(): pl.pallas_call(kernel, out_shape=(jax.ShapeDtypeStruct((4, OWN, NY, NZ),...  56.7 us
    unnamed x3, local copies, waits for them, and re-layouts  1.95 us

profile of v4, /device:TPU:2, one launch (start us, length us, event | category | flops | bytes accessed | tf_op | source)
XLA Modules:
  0.0 59.3 jit_solution(14332682206769044972)
XLA Ops:
  0.6 56.7 %shard_map.49 = (f32[4,8,32,128]{3,2,1,0:T(8,128)S(1)}, f32[4,16]{1,0:T(4,128)S(1)}, f32[4,16]{1,0:T(4,128)S(1)}) custom-call(f32[4,8,32,128]{3,2,1,0:T(8,128)} %orbitals.1, f32[8,32,128]{2,1,0:T(8,128)} %potential.1), custom_call_target="tpu_custom_call" | custom-call | tf_op jit(solution)/shard_map/pallas_call | solution.py:372
  57.4 0.8 %copy.8 = f32[4,8,32,128]{3,2,1,0:T(8,128)} copy(f32[4,8,32,128]{3,2,1,0:T(8,128)S(1)} %get-tuple-element.6) | data formatting | bytes 1048576
  58.2 0.6 copy.9
  58.7 0.6 copy.10

commit v5 on v4

--- a/solution.py
+++ b/solution.py
@@ -56,7 +56,7 @@
     return total
 
 
-def kernel(orbitals, potential, filtered, corr, ham,
+def kernel(orbitals, potential, filtered, grams,
            p0, p1, p2, p3, p4, hy, v_ref, every, acc, rows,
            in_sem, v_send, v_recv, a_send, a_recv, b_send, b_recv, c_send, c_recv,
            x_send, x_recv, out_sem, r_send, r_recv, met):
@@ -347,10 +347,8 @@
     start(sum_copies)
     arrived(sum_copies)
     total = jnp.sum(rows[...], axis=0, keepdims=True)
-    for kind, ref in ((0, corr), (1, ham)):
-        for i in range(4):
-            first = (kind * 4 + i) * 16
-            ref[pl.ds(i, 1), :] = total[:, first : first + 16]
+    for i in range(8):
+        grams[pl.ds(i, 1), :] = total[:, 16 * i : 16 * i + 16]
 
     for copies in [v_copies, v_shared, sum_copies] + a_copies + b_copies + c_copies + x_copies:
         if not any(copies is other for other in gone):
@@ -369,17 +367,15 @@
     orbitals, potential = (pltpu.with_memory_space_constraint(value, pltpu.HBM) for value in (orbitals, potential))
     dma = pltpu.SemaphoreType.DMA
     field = lambda count: pltpu.VMEM((4, count, NY, NZ), jnp.float32)
-    return pl.pallas_call(
+    filtered, grams = pl.pallas_call(
         kernel,
         out_shape=(
             jax.ShapeDtypeStruct((4, OWN, NY, NZ), jnp.float32),
-            jax.ShapeDtypeStruct((4, 16), jnp.float32),
-            jax.ShapeDtypeStruct((4, 16), jnp.float32),
+            jax.ShapeDtypeStruct((8, 16), jnp.float32),
         ),
         in_specs=[pl.BlockSpec(memory_space=pltpu.HBM)] * 2,
         out_specs=(
             pl.BlockSpec(memory_space=pl.ANY),
-            pl.BlockSpec(memory_space=pltpu.VMEM),
             pl.BlockSpec(memory_space=pltpu.VMEM),
         ),
         scratch_shapes=[
@@ -397,6 +393,7 @@
             collective_id=0, has_side_effects=True, vmem_limit_bytes=40 * 1024 * 1024
         ),
     )(orbitals, potential)
+    return filtered, grams[0:4], grams[4:8]
 
 
 def solution(mesh):

time: 59.7 us -> 59.1 us (0.990)
    unnamed x3 -> x1, local copies, waits for them, and re-layouts: 1.95 us -> 0.79 us
where the time goes in v5:
time: 59.1 us; the launch traced here: 58.7 us
  Pallas kernels  56.7 us (96%)
  local copies, waits for them, and re-layouts  1.38 us (2%)
  between operations  0.64 us (1%)
    pallas_call x1, Pallas kernels, per_device(): pl.pallas_call(kernel, out_shape=(jax.ShapeDtypeStruct((4, OWN, NY, NZ),...  56.7 us

profile of v5, /device:TPU:2, one launch (start us, length us, event | category | flops | bytes accessed | tf_op | source)
XLA Modules:
  0.0 58.7 jit_solution(16375967567220989252)
XLA Ops:
  0.6 56.7 %shard_map.49 = (f32[4,8,32,128]{3,2,1,0:T(8,128)S(1)}, f32[8,16]{1,0:T(8,128)S(1)}) custom-call(f32[4,8,32,128]{3,2,1,0:T(8,128)} %orbitals.1, f32[8,32,128]{2,1,0:T(8,128)} %potential.1), custom_call_target="tpu_custom_call" | custom-call | tf_op jit(solution)/shard_map/pallas_call | solution.py:370
  57.4 0.6 fusion
  58.0 0.8 %copy.6 = f32[4,8,32,128]{3,2,1,0:T(8,128)} copy(f32[4,8,32,128]{3,2,1,0:T(8,128)S(1)} %get-tuple-element.12) | data formatting | bytes 1048576
